TPU v7x, 128 devices: a whole 4x4x4 slice. The times are simulated.
128 devices in a mesh: expert: 64 (over z, y, x_hi, core), dp: 2 (over x_lo).
Axes of the slice: x: 4 (x_hi: 2, x_lo: 2; x = x_hi * 2 + x_lo), y: 4, z: 4, core: 2. Of those that a mesh axis runs over, the one named last changes fastest.
Arguments:
- activations: bfloat16 [16384, 3584], P(('expert', 'dp')), may hold values from -6 to 6
- out_grad: bfloat16 [16384, 3584], P(('expert', 'dp')), may hold values from -1.5 to 1.5
- expert_ids: int32 [16384, 1], P(('expert', 'dp')), may hold values from 0 to 63; in each aligned block of 128 rows (0 to 127, 128 to 255, ...) at most 6 rows name the same one
- gate_probs: bfloat16 [16384, 1], P(('expert', 'dp')), may hold values from 0.049804688 to 1
- gate_weight: bfloat16 [64, 3584, 1024], P('expert', 'dp'), may hold values from -0.09375 to 0.09375
- up_weight: bfloat16 [64, 3584, 1024], P('expert', 'dp'), may hold values from -0.09375 to 0.09375
- down_weight: bfloat16 [64, 3584, 1024], P('expert', 'dp'), may hold values from -0.1875 to 0.1875
Outputs:
- input_delta: bfloat16 [16384, 3584], P(('expert', 'dp'))
- prob_delta: bfloat16 [16384, 1], P(('expert', 'dp'))
- gate_delta: bfloat16 [64, 3584, 1024], P('expert', 'dp')
- up_delta: bfloat16 [64, 3584, 1024], P('expert', 'dp')
- down_delta: bfloat16 [64, 3584, 1024], P('expert', 'dp')
Inputs may be any that keep to these rules, and one draw needn't show every extreme that they name: `expert_ids`: among the 128 tokens of one device (aligned blocks of rows), no expert is named more than 6 times, a bound that some block reaches.
All inputs are finite; a program needn't handle non-finite values.
Results may differ from a plain program's by a relative error of at most 0.034.
Values may be sent and summed in bfloat16 or wider, within the bound.
A program may use at most 128 MiB of HBM per device.

v0:
```python
import jax
import jax.numpy as jnp
from jax import lax
from jax.sharding import PartitionSpec as P


def activate(summed, prob_rows, hidden):
    pre_gate = summed[:, :hidden]
    pre_up = summed[:, hidden : 2 * hidden]
    raw_grad = summed[:, 2 * hidden :]
    sigmoid_gate = jax.nn.sigmoid(pre_gate)
    silu_gate = pre_gate * sigmoid_gate
    hidden_rows = (silu_gate * pre_up).astype(jnp.bfloat16)
    scaled_grad = prob_rows.astype(jnp.float32)[:, None] * raw_grad
    slope = sigmoid_gate * (1.0 + pre_gate * (1.0 - sigmoid_gate))
    gate_rows = (scaled_grad * pre_up * slope).astype(jnp.bfloat16)
    up_rows = (scaled_grad * silu_gate).astype(jnp.bfloat16)
    return (hidden_rows, gate_rows, up_rows)


def on_device(activations, out_grad, expert_ids, gate_probs, gate_weight, up_weight, down_weight):
    expert_count = lax.axis_size("expert")
    group_size = lax.axis_size("dp")
    token_count = activations.shape[0]
    feature_width = activations.shape[1]
    routes_each = expert_ids.shape[1]
    capacity = max(2, 3 * token_count * routes_each // expert_count)
    slab_rows = expert_count * capacity
    group_rows = slab_rows * group_size
    w_gate = gate_weight[0]
    w_up = up_weight[0]
    w_down = down_weight[0]
    hidden = w_gate.shape[1]
    routes = expert_ids[:, 0]
    onehot = (routes[:, None] == jnp.arange(expert_count, dtype=jnp.int32)[None, :]).astype(
        jnp.int32
    )
    earlier = jnp.cumsum(onehot, axis=0) - onehot
    slot_index = jnp.sum(earlier * onehot, axis=1)
    target = routes * capacity + slot_index
    source = (
        jnp.zeros((slab_rows,), jnp.int32).at[target].set(jnp.arange(token_count, dtype=jnp.int32))
    )
    filled = jnp.zeros((slab_rows,), jnp.bool_).at[target].set(True)
    slot_probs = jnp.where(filled, gate_probs[source, 0], 0)
    send_tokens = jnp.where(filled[:, None], activations[source], 0)
    send_grads = jnp.where(filled[:, None], out_grad[source], 0)
    arrived_tokens, arrived_grads, arrived_probs = (
        lax.all_to_all(
            send_tokens.reshape(expert_count, capacity, feature_width),
            "expert",
            split_axis=0,
            concat_axis=0,
            tiled=True,
        ),
        lax.all_to_all(
            send_grads.reshape(expert_count, capacity, feature_width),
            "expert",
            split_axis=0,
            concat_axis=0,
            tiled=True,
        ),
        lax.all_to_all(
            slot_probs.reshape(expert_count, capacity),
            "expert",
            split_axis=0,
            concat_axis=0,
            tiled=True,
        ),
    )
    own_tokens = arrived_tokens.reshape(slab_rows, feature_width)
    own_grads = arrived_grads.reshape(slab_rows, feature_width)
    spread_probs = jnp.broadcast_to(arrived_probs.reshape(slab_rows, 1), (slab_rows, group_size))
    group_tokens, group_grads, group_spread = (
        lax.all_to_all(own_tokens, "dp", split_axis=1, concat_axis=0, tiled=True),
        lax.all_to_all(own_grads, "dp", split_axis=1, concat_axis=0, tiled=True),
        lax.all_to_all(spread_probs, "dp", split_axis=1, concat_axis=0, tiled=True),
    )
    group_probs = group_spread.reshape(group_rows)
    first_row = lax.axis_index("dp") * slab_rows
    own_probs = lax.dynamic_slice_in_dim(group_probs, first_row, slab_rows, 0)
    row_tokens = group_tokens
    row_grads = group_grads
    own_sums = lax.psum_scatter(
        jnp.concatenate(
            [
                jnp.dot(row_tokens, w_gate, preferred_element_type=jnp.float32),
                jnp.dot(row_tokens, w_up, preferred_element_type=jnp.float32),
                jnp.dot(row_grads, w_down, preferred_element_type=jnp.float32),
            ],
            axis=1,
        ).astype(jnp.bfloat16),
        "dp",
        scatter_dimension=0,
        tiled=True,
    ).astype(jnp.float32)
    own_hidden, gate_rows, up_rows = activate(own_sums, own_probs, hidden)
    hidden_rows = lax.all_gather(own_hidden, "dp", axis=0, tiled=True)
    accumulate_gate_rows = lax.all_gather(gate_rows, "dp", axis=0, tiled=True)
    accumulate_up_rows = lax.all_gather(up_rows, "dp", axis=0, tiled=True)
    prob_rows = lax.all_gather(own_probs, "dp", axis=0, tiled=True)
    row_tokens = group_tokens
    row_grads = group_grads
    scaled = (prob_rows.astype(jnp.float32)[:, None] * hidden_rows.astype(jnp.float32)).astype(
        jnp.bfloat16
    )
    new_gate = jnp.einsum(
        "rd,rf->df", row_tokens, accumulate_gate_rows, preferred_element_type=jnp.float32
    )
    new_up = jnp.einsum(
        "rd,rf->df", row_tokens, accumulate_up_rows, preferred_element_type=jnp.float32
    )
    new_down = jnp.einsum("rd,rf->df", row_grads, scaled, preferred_element_type=jnp.float32)
    back_rows = jnp.einsum(
        "rf,df->rd", accumulate_gate_rows, w_gate, preferred_element_type=jnp.float32
    )
    back_rows = back_rows + jnp.einsum(
        "rf,df->rd", accumulate_up_rows, w_up, preferred_element_type=jnp.float32
    )
    output_rows = jnp.einsum("rf,df->rd", hidden_rows, w_down, preferred_element_type=jnp.float32)
    inner_terms = jnp.sum(row_grads.astype(jnp.float32) * output_rows, axis=1)
    prob_terms = lax.psum_scatter(inner_terms, "dp", scatter_dimension=0, tiled=True)
    prob_rounded = prob_terms.astype(jnp.bfloat16)
    back_rounded = back_rows.astype(jnp.bfloat16)
    returned_rows = lax.all_to_all(back_rounded, "dp", split_axis=0, concat_axis=1, tiled=True)
    final_rows, final_probs = (
        lax.all_to_all(
            returned_rows.reshape(expert_count, capacity, feature_width),
            "expert",
            split_axis=0,
            concat_axis=0,
            tiled=True,
        ),
        lax.all_to_all(
            prob_rounded.reshape(expert_count, capacity),
            "expert",
            split_axis=0,
            concat_axis=0,
            tiled=True,
        ),
    )
    input_delta = final_rows.reshape(slab_rows, feature_width)[target]
    prob_delta = final_probs.reshape(slab_rows)[target][:, None]
    return (
        input_delta,
        prob_delta,
        new_gate.astype(jnp.bfloat16)[None],
        new_up.astype(jnp.bfloat16)[None],
        new_down.astype(jnp.bfloat16)[None],
    )


def solution(mesh):
    return jax.shard_map(
        on_device,
        mesh=mesh,
        in_specs=(
            P(("expert", "dp"), None),
            P(("expert", "dp"), None),
            P(("expert", "dp"), None),
            P(("expert", "dp"), None),
            P("expert", "dp", None),
            P("expert", "dp", None),
            P("expert", "dp", None),
        ),
        out_specs=(
            P(("expert", "dp"), None),
            P(("expert", "dp"), None),
            P("expert", "dp", None),
            P("expert", "dp", None),
            P("expert", "dp", None),
        ),
        check_vma=False,
    )
```

profile of v0, /device:TPU:52, one launch (start us, length us, event | category | flops | bytes accessed | tf_op | source)
XLA Modules:
  0.0 543.7 jit_solution(1405030936872476756)
XLA Ops:
  35.3 54.0 %all_to_all.102 = bf16[64,6,3584]{2,1,0:T(8,128)(2,1)} all-to-all(bf16[64,6,3584]{2,1,0:T(8,128)(2,1)S(1)} %get-tuple-element.10), channel_id=1, replica_groups=mesh['expert'=64,'dp'=2] {'expert'}, dimensions={0} | all-to-all | bytes 5505024 | tf_op jit(solution)/shard_map/all_to_all | solution.py:49
  89.2 10.3 %all-to-all-start.4 = ((bf16[64,6,3584]{2,1,0:T(8,128)(2,1)}), bf16[64,6,3584]{2,1,0:T(8,128)(2,1)}, u32[]{:S(2)}, u32[]{:S(2)}) async-start(bf16[64,6,3584]{2,1,0:T(8,128)(2,1)} %get-tuple-element.11), calls=%async_computation.4 | async-start | bytes 7340032 | tf_op jit(solution)/shard_map/all_to_all | solution.py:56
  99.6 7.3 %all_to_all.76 = bf16[384,2,1792]{2,1,0:T(2,128)(2,1)} reshape(bf16[64,6,3584]{2,1,0:T(8,128)(2,1)} %all_to_all.102) | data formatting | bytes 5505024 | tf_op jit(solution)/shard_map/all_to_all | solution.py:75
  110.4 37.4 %all-to-all-done.4 = bf16[64,6,3584]{2,1,0:T(8,128)(2,1)} async-done(((bf16[64,6,3584]{2,1,0:T(8,128)(2,1)}), bf16[64,6,3584]{2,1,0:T(8,128)(2,1)}, u32[]{:S(2)}, u32[]{:S(2)}) %all-to-all-start.4) | async-done | bytes 2752544 | tf_op jit(solution)/shard_map/all_to_all | solution.py:56
  153.0 7.3 %all_to_all.81 = bf16[384,2,1792]{2,1,0:T(2,128)(2,1)} reshape(bf16[64,6,3584]{2,1,0:T(8,128)(2,1)} %all-to-all-done.4) | data formatting | bytes 5505024 | tf_op jit(solution)/shard_map/all_to_all | solution.py:76
  163.9 22.1 %all-to-all-done.3 = bf16[384,2,1792]{2,0,1:T(8,128)(2,1)} async-done(((bf16[384,2,1792]{2,0,1:T(8,128)(2,1)}), bf16[384,2,1792]{2,0,1:T(8,128)(2,1)}, u32[]{:S(2)}, u32[]{:S(2)}) %all-to-all-start.3) | async-done | bytes 2752544 | tf_op jit(solution)/shard_map/all_to_all | solution.py:75
  203.3 19.9 %all-to-all-done.5 = bf16[384,2,1792]{2,0,1:T(8,128)(2,1)} async-done(((bf16[384,2,1792]{2,0,1:T(8,128)(2,1)}), bf16[384,2,1792]{2,0,1:T(8,128)(2,1)}, u32[]{:S(2)}, u32[]{:S(2)}) %all-to-all-start.5) | async-done | bytes 2752544 | tf_op jit(solution)/shard_map/all_to_all | solution.py:76
  235.1 13.5 %all_to_all.103 = bf16[64,1,6]{2,1,0:T(2,128)(2,1)S(1)} all-to-all(bf16[64,1,6]{2,1,0:T(2,128)(2,1)S(1)} %all_to_all.91), channel_id=1, replica_groups=mesh['expert'=64,'dp'=2] {'expert'}, dimensions={0} | all-to-all | bytes 1536 | tf_op jit(solution)/shard_map/all_to_all | solution.py:63
  257.9 36.4 %reduce-scatter.2.cloned.1.call-done = bf16[384,3072]{1,0:T(8,128)(2,1)} async-done(((bf16[768,3072]{1,0:T(8,128)(2,1)}), bf16[384,3072]{1,0:T(8,128)(2,1)}) %reduce-scatter.2.cloned.1.call-update) | async-done | bytes 2359312 | tf_op jit(solution)/shard_map/reduce_scatter | solution.py:84
  300.4 29.5 %all-gather.7.cloned.1.call-done = bf16[768,1024]{1,0:T(8,128)(2,1)} async-done(((bf16[384,1024]{1,0:T(8,128)(2,1)}), bf16[768,1024]{1,0:T(8,128)(2,1)}) %all-gather.7.cloned.1.call-update) | async-done | bytes 1572880 | tf_op jit(solution)/shard_map/all_gather | solution.py:100
  329.9 8.0 %fusion.3 = f32[768,1792]{1,0:T(8,128)} fusion(bf16[768,1024]{1,0:T(8,128)(2,1)} %all-gather.7.cloned.1.call-done, bf16[1,1792,1024]{2,1,0:T(8,128)(2,1)} %param.12), kind=kOutput, calls=%fused_computation.16 | convolution fusion | flops 2818572288 | bytes 10747904 | tf_op jit(solution)/shard_map/rf,df->rd/dot_general | solution.py:117
  337.9 25.1 %all-gather.5.cloned.1.call-done = bf16[768,1024]{1,0:T(8,128)(2,1)} async-done(((bf16[384,1024]{1,0:T(8,128)(2,1)}), bf16[768,1024]{1,0:T(8,128)(2,1)}) %all-gather.5.cloned.1.call-update) | async-done | bytes 1572880 | tf_op jit(solution)/shard_map/all_gather | solution.py:99
  363.0 8.7 %add_convert_fusion = bf16[768,1792]{1,0:T(8,128)(2,1)} fusion(f32[768,1792]{1,0:T(8,128)} %fusion.3, bf16[768,1024]{1,0:T(8,128)(2,1)} %all-gather.5.cloned.1.call-done, bf16[1,1792,1024]{2,1,0:T(8,128)(2,1)} %param.11), kind=kOutput, calls=%fused_computation.8 | convolution fusion | flops 2821324800 | bytes 13500416 | tf_op jit(solution)/shard_map/rf,df->rd/dot_general | solution.py:114
  378.2 33.9 %all-gather.9.cloned.1.call-done = bf16[768,1024]{1,0:T(8,128)(2,1)} async-done(((bf16[384,1024]{1,0:T(8,128)(2,1)}), bf16[768,1024]{1,0:T(8,128)(2,1)}) %all-gather.9.cloned.1.call-update) | async-done | bytes 1572880 | tf_op jit(solution)/shard_map/all_gather | solution.py:98
  412.1 6.5 %multiply_reduce_fusion = f32[768]{0:T(1024)S(1)} fusion(bf16[768,1792]{1,0:T(8,128)(2,1)} %bitcast.10, bf16[768,1024]{1,0:T(8,128)(2,1)} %all-gather.9.cloned.1.call-done, bf16[1,1792,1024]{2,1,0:T(8,128)(2,1)} %param.13), kind=kOutput, calls=%fused_computation.7 | convolution fusion | flops 2822700288 | bytes 7998464 | tf_op jit(solution)/shard_map/rf,df->rd/dot_general | solution.py:120
  418.6 6.7 %all-reduce.1 = bf16[768]{0:T(1024)(128)(2,1)S(1)} all-reduce(f32[768]{0:T(1024)S(1)} %multiply_reduce_fusion), channel_id=3, replica_groups=mesh['expert'=64,'dp'=2] {'dp'}, use_global_device_ids=true, to_apply=%region_6.7.clone | all-reduce | flops 768 | bytes 4608
  426.1 10.6 %all-to-all-start.8 = ((bf16[64,1,6]{2,1,0:T(2,128)(2,1)}), bf16[64,1,6]{2,1,0:T(2,128)(2,1)S(1)}, u32[]{:S(2)}, u32[]{:S(2)}) async-start(bf16[64,1,6]{2,1,0:T(2,128)(2,1)} %all_to_all.92), calls=%async_computation.9 | async-start | bytes 65536 | tf_op jit(solution)/shard_map/all_to_all | solution.py:134
  436.8 6.1 %copy.18 = bf16[384,2,1792]{2,1,0:T(2,128)(2,1)} copy(bf16[384,2,1792]{2,0,1:T(8,128)(2,1)} %bitcast.13) | data formatting | bytes 5505024 | tf_op jit(solution)/shard_map/all_to_all | solution.py:125
  442.9 7.6 %reshape.76 = bf16[64,6,3584]{2,1,0:T(8,128)(2,1)} reshape(bf16[384,2,1792]{2,1,0:T(2,128)(2,1)} %copy.18) | data formatting | bytes 5505024 | tf_op jit(solution)/shard_map/reshape | solution.py:128
  450.5 10.6 %all-to-all-start.7 = ((bf16[64,6,3584]{2,1,0:T(8,128)(2,1)}), bf16[64,6,3584]{2,1,0:T(8,128)(2,1)}, u32[]{:S(2)}, u32[]{:S(2)}) async-start(bf16[64,6,3584]{2,1,0:T(8,128)(2,1)} %reshape.76), calls=%async_computation.8 | async-start | bytes 7340032 | tf_op jit(solution)/shard_map/all_to_all | solution.py:127
  461.2 43.8 %all-gather = bf16[2,1,384]{2,1,0:T(2,128)(2,1)S(1)} all-gather(bf16[1,1,384]{2,1,0:T(2,128)(2,1)S(1)} %reshape.141), channel_id=1, replica_groups=mesh['expert'=64,'dp'=2] {'dp'}, dimensions={0}, use_global_device_ids=true | all-gather | bytes 2304 | tf_op jit(solution)/shard_map/all_gather | solution.py:101
  505.1 6.4 %fusion.12 = bf16[1,1792,1024]{2,1,0:T(8,128)(2,1)} fusion(bf16[768,1792]{1,0:T(8,128)(2,1)} %bitcast.5, bf16[768,1024]{1,0:T(8,128)(2,1)S(1)} %copy-done.6), kind=kOutput, calls=%fused_computation.27 | convolution fusion | flops 2820407296 | bytes 7995392 | tf_op jit(solution)/shard_map/rd,rf->df/dot_general | solution.py:110
  511.5 6.4 %fusion.11 = bf16[1,1792,1024]{2,1,0:T(8,128)(2,1)} fusion(bf16[768,1792]{1,0:T(8,128)(2,1)} %bitcast.5, bf16[768,1024]{1,0:T(8,128)(2,1)S(1)} %copy-done.7), kind=kOutput, calls=%fused_computation.26 | convolution fusion | flops 2820407296 | bytes 7995392 | tf_op jit(solution)/shard_map/rd,rf->df/dot_general | solution.py:107
  517.9 6.4 %fusion.13 = bf16[1,1792,1024]{2,1,0:T(8,128)(2,1)} fusion(bf16[768,1792]{1,0:T(8,128)(2,1)} %bitcast.10, bf16[768,1024]{1,0:T(8,128)(2,1)S(1)} %copy-done.8, f32[768]{0:T(1024)S(1)} %reshape.143), kind=kOutput, calls=%fused_computation.28 | convolution fusion | flops 2822766592 | bytes 7998464 | tf_op jit(solution)/shard_map/rd,rf->df/dot_general | solution.py:113
  (85 shorter events, 104.0 us)
Async XLA Ops:
  7.2 3.5 copy-start
  14.6 5.5 %copy-start.3 = (bf16[128,3584]{1,0:T(8,128)(2,1)S(1)}, bf16[128,3584]{1,0:T(8,128)(2,1)}, u32[]{:S(2)}) copy-start(bf16[128,3584]{1,0:T(8,128)(2,1)} %param.8) | copy-start | bytes 2752516
  89.2 58.7 %all-to-all-start.4 = ((bf16[64,6,3584]{2,1,0:T(8,128)(2,1)}), bf16[64,6,3584]{2,1,0:T(8,128)(2,1)}, u32[]{:S(2)}, u32[]{:S(2)}) async-start(bf16[64,6,3584]{2,1,0:T(8,128)(2,1)} %get-tuple-element.11), calls=%async_computation.4 | async-start | bytes 7340032 | tf_op jit(solution)/shard_map/all_to_all | solution.py:56
  147.9 38.1 %all-to-all-start.3 = ((bf16[384,2,1792]{2,0,1:T(8,128)(2,1)}), bf16[384,2,1792]{2,0,1:T(8,128)(2,1)}, u32[]{:S(2)}, u32[]{:S(2)}) async-start(bf16[384,2,1792]{2,0,1:T(8,128)(2,1)} %copy.16), calls=%async_computation.3 | async-start | bytes 5505024 | tf_op jit(solution)/shard_map/all_to_all | solution.py:75
  186.0 37.3 %all-to-all-start.5 = ((bf16[384,2,1792]{2,0,1:T(8,128)(2,1)}), bf16[384,2,1792]{2,0,1:T(8,128)(2,1)}, u32[]{:S(2)}, u32[]{:S(2)}) async-start(bf16[384,2,1792]{2,0,1:T(8,128)(2,1)} %copy.17), calls=%async_computation.5 | async-start | bytes 5505024 | tf_op jit(solution)/shard_map/all_to_all | solution.py:76
  191.1 103.3 %reduce-scatter.2.cloned.1.call-start = ((), (), s32[]{:S(2)}) async-start(), calls=%async_computation.10 | async-start | bytes 7077888 | tf_op jit(solution)/shard_map/reduce_scatter | solution.py:84
  191.4 6.0 %copy-start.5 = (bf16[1,1792,1024]{2,1,0:T(8,128)(2,1)S(1)}, bf16[1,1792,1024]{2,1,0:T(8,128)(2,1)}, u32[]{:S(2)}) copy-start(bf16[1,1792,1024]{2,1,0:T(8,128)(2,1)} %param.12) | copy-start | bytes 11010052
  223.3 6.0 %copy-start.4 = (bf16[768,1024]{1,0:T(8,128)(2,1)S(1)}, bf16[768,1024]{1,0:T(8,128)(2,1)}, u32[]{:S(2)}) copy-start(bf16[768,1024]{1,0:T(8,128)(2,1)} %fusion.19) | copy-start | bytes 4718596
  231.6 0.7 copy-start.2
  250.7 7.0 %all-to-all-start.1 = ((bf16[2,2,192]{2,1,0:T(2,128)(2,1)}), bf16[2,2,192]{2,1,0:T(2,128)(2,1)S(1)}, u32[]{:S(2)}, u32[]{:S(2)}) async-start(bf16[2,2,192]{2,1,0:T(2,128)(2,1)} %reshape.153), calls=%async_computation.1 | async-start | bytes 4096 | tf_op jit(solution)/shard_map/all_to_all | solution.py:77
  253.9 76.0 %all-gather.7.cloned.1.call-start = ((), (), s32[]{:S(2)}) async-start(), calls=%async_computation.12 | async-start | bytes 2359296 | tf_op jit(solution)/shard_map/all_gather | solution.py:100
  299.1 63.9 %all-gather.5.cloned.1.call-start = ((), (), s32[]{:S(2)}) async-start(), calls=%async_computation.11 | async-start | bytes 2359296 | tf_op jit(solution)/shard_map/all_gather | solution.py:99
  299.8 112.3 %all-gather.9.cloned.1.call-start = ((), (), s32[]{:S(2)}) async-start(), calls=%async_computation.13 | async-start | bytes 2359296 | tf_op jit(solution)/shard_map/all_gather | solution.py:98
  371.7 5.2 copy-start.9
  371.7 54.4 %all-to-all-start.6 = ((bf16[2,384,1792]{2,1,0:T(8,128)(2,1)}), bf16[2,384,1792]{2,1,0:T(8,128)(2,1)}, u32[]{:S(2)}, u32[]{:S(2)}) async-start(bf16[2,384,1792]{2,1,0:T(8,128)(2,1)} %bitcast.63), calls=%async_computation.7 | async-start | bytes 5505024 | tf_op jit(solution)/shard_map/all_to_all | solution.py:125
  426.1 24.4 %all-to-all-start.8 = ((bf16[64,1,6]{2,1,0:T(2,128)(2,1)}), bf16[64,1,6]{2,1,0:T(2,128)(2,1)S(1)}, u32[]{:S(2)}, u32[]{:S(2)}) async-start(bf16[64,1,6]{2,1,0:T(2,128)(2,1)} %all_to_all.92), calls=%async_computation.9 | async-start | bytes 65536 | tf_op jit(solution)/shard_map/all_to_all | solution.py:134
  450.5 54.5 %copy-start.6 = (bf16[768,1024]{1,0:T(8,128)(2,1)S(1)}, bf16[768,1024]{1,0:T(8,128)(2,1)}, u32[]{:S(2)}) copy-start(bf16[768,1024]{1,0:T(8,128)(2,1)} %all-gather.7.cloned.1.call-done) | copy-start | bytes 4718596
  450.5 75.8 %all-to-all-start.7 = ((bf16[64,6,3584]{2,1,0:T(8,128)(2,1)}), bf16[64,6,3584]{2,1,0:T(8,128)(2,1)}, u32[]{:S(2)}, u32[]{:S(2)}) async-start(bf16[64,6,3584]{2,1,0:T(8,128)(2,1)} %reshape.76), calls=%async_computation.8 | async-start | bytes 7340032 | tf_op jit(solution)/shard_map/all_to_all | solution.py:127
  505.0 6.4 %copy-start.7 = (bf16[768,1024]{1,0:T(8,128)(2,1)S(1)}, bf16[768,1024]{1,0:T(8,128)(2,1)}, u32[]{:S(2)}) copy-start(bf16[768,1024]{1,0:T(8,128)(2,1)} %all-gather.5.cloned.1.call-done) | copy-start | bytes 4718596
  511.5 6.4 %copy-start.8 = (bf16[768,1024]{1,0:T(8,128)(2,1)S(1)}, bf16[768,1024]{1,0:T(8,128)(2,1)}, u32[]{:S(2)}) copy-start(bf16[768,1024]{1,0:T(8,128)(2,1)} %all-gather.9.cloned.1.call-done) | copy-start | bytes 4718596
  526.3 10.7 %copy-start.1 = (bf16[128,3584]{1,0:T(8,128)(2,1)S(1)}, bf16[128,3584]{1,0:T(8,128)(2,1)}, u32[]{:S(2)}) copy-start(bf16[128,3584]{1,0:T(8,128)(2,1)} %param.7) | copy-start | bytes 2752516
Sparse Core Ops, SparseCore 0:
  231.7 62.5 reduce-scatter.1
  299.2 30.6 all-gather.6
  332.2 30.6 all-gather.4
  365.1 46.8 all-gather.8
where the time goes:
time: 553 us; the launch traced here: 544 us
  waiting for transfers between devices  209 us (38%)
  blocking collectives  118 us (21%)
  local copies, waits for them, and re-layouts  75.1 us (14%)
  matrix products  60.3 us (11%)
  starting transfers between devices  51.2 us (9%)
  other arithmetic  15.3 us (3%)
  between operations  14.9 us (3%)
    all_to_all x1, blocking collectives, on_device(): lax.all_to_all(send_tokens.reshape(expert_count, capacity, feature_width)...  54 us
    all_gather x1, blocking collectives, on_device(): prob_rows = lax.all_gather(own_probs, 'dp', axis=0, tiled=True)  43.8 us
    all_to_all x1, waiting for transfers between devices, on_device(): lax.all_to_all(send_grads.reshape(expert_count, capacity, feature_width),...  37.4 us
    reduce_scatter x1, waiting for transfers between devices, on_device(): lax.psum_scatter(jnp.concatenate([jnp.dot(row_tokens, w_gate, preferred_e...  36.4 us
    all_gather x1, waiting for transfers between devices, on_device(): hidden_rows = lax.all_gather(own_hidden, 'dp', axis=0, tiled=True)  33.9 us
    all_gather x1, waiting for transfers between devices, on_device(): accumulate_up_rows = lax.all_gather(up_rows, 'dp', axis=0, tiled=True)  29.5 us
    all_gather x1, waiting for transfers between devices, on_device(): accumulate_gate_rows = lax.all_gather(gate_rows, 'dp', axis=0, tiled=True)  25.1 us
    all_to_all x1, waiting for transfers between devices, on_device(): lax.all_to_all(own_tokens, 'dp', split_axis=1, concat_axis=0, tiled=True)  22.1 us
  transfers between devices with their start and end apart: 11, of which 8 were waited for; matrix products, arithmetic and copies ran while one was open for 15% of the time, Pallas kernels for 0%

commit v1 on v0

--- a/solution.py
+++ b/solution.py
@@ -96,7 +96,9 @@
     ).astype(jnp.float32)
     own_hidden, gate_rows, up_rows = activate(own_sums, own_probs, hidden)
     hidden_rows = lax.all_gather(own_hidden, "dp", axis=0, tiled=True)
-    accumulate_gate_rows = lax.all_gather(gate_rows, "dp", axis=0, tiled=True)
+    accumulate_gate_rows = jnp.concatenate(
+        lax.all_to_all(jnp.stack([gate_rows] * lax.axis_size("dp")), "dp", 0, 0), axis=0
+    )
     accumulate_up_rows = lax.all_gather(up_rows, "dp", axis=0, tiled=True)
     prob_rows = lax.all_gather(own_probs, "dp", axis=0, tiled=True)
     row_tokens = group_tokens

time: 553 us -> 529 us (0.957)
  waiting for transfers between devices: 209 us -> 169 us
  local copies, waits for them, and re-layouts: 75.1 us -> 84.6 us
  blocking collectives: 118 us -> 125 us
    all_gather x1 -> x0, waiting for transfers between devices: 25.1 us -> none  [on_device(): accumulate_gate_rows = lax.all_gather(gate_rows, 'dp', axis=0, tiled=True)]
    all_gather x1, waiting for transfers between devices: 33.9 us -> 20.8 us  [on_device(): hidden_rows = lax.all_gather(own_hidden, 'dp', axis=0, tiled=True)]
    all_to_all x2 -> x3, local copies, waits for them, and re-layouts: 10.9 us -> 20.3 us  [on_device(): lax.all_to_all(own_tokens, 'dp', split_axis=1, concat_axis=0, tiled=True)]
    unnamed x1, blocking collectives: 6.72 us -> 13.4 us
    all_gather x1, waiting for transfers between devices: 29.5 us -> 35.8 us  [on_device(): accumulate_up_rows = lax.all_gather(up_rows, 'dp', axis=0, tiled=True)]
  transfers between devices with their start and end apart: 11 -> 11, of which waited for: 8 -> 7; matrix products, arithmetic and copies ran while one was open for 15% -> 17% of each run, Pallas kernels for 0% -> 0%
where the time goes in v1:
time: 529 us; the launch traced here: 519 us
  waiting for transfers between devices  169 us (32%)
  blocking collectives  125 us (24%)
  local copies, waits for them, and re-layouts  84.6 us (16%)
  matrix products  55.1 us (10%)
  starting transfers between devices  54.7 us (10%)
  other arithmetic  16.3 us (3%)
  between operations  14.9 us (3%)
    all_to_all x1, blocking collectives, on_device(): lax.all_to_all(send_tokens.reshape(expert_count, capacity, feature_width)...  54 us
    all_gather x1, blocking collectives, on_device(): prob_rows = lax.all_gather(own_probs, 'dp', axis=0, tiled=True)  43.8 us
    reduce_scatter x1, waiting for transfers between devices, on_device(): lax.psum_scatter(jnp.concatenate([jnp.dot(row_tokens, w_gate, preferred_e...  36.4 us
    all_gather x1, waiting for transfers between devices, on_device(): accumulate_up_rows = lax.all_gather(up_rows, 'dp', axis=0, tiled=True)  35.8 us
    all_to_all x1, waiting for transfers between devices, on_device(): lax.all_to_all(send_grads.reshape(expert_count, capacity, feature_width),...  32.5 us
    all_to_all x1, waiting for transfers between devices, on_device(): lax.all_to_all(own_tokens, 'dp', split_axis=1, concat_axis=0, tiled=True)  22.1 us
    all_gather x1, waiting for transfers between devices, on_device(): hidden_rows = lax.all_gather(own_hidden, 'dp', axis=0, tiled=True)  20.8 us
    all_to_all x3, local copies, waits for them, and re-layouts, on_device(): lax.all_to_all(own_tokens, 'dp', split_axis=1, concat_axis=0, tiled=True)  20.3 us
  transfers between devices with their start and end apart: 11, of which 7 were waited for; matrix products, arithmetic and copies ran while one was open for 17% of the time, Pallas kernels for 0%

profile of v1, /device:TPU:52, one launch (start us, length us, event | category | flops | bytes accessed | tf_op | source)
XLA Modules:
  0.0 519.3 jit_solution(1841694939668939408)
XLA Ops:
  35.3 54.0 %all_to_all.107 = bf16[64,6,3584]{2,1,0:T(8,128)(2,1)} all-to-all(bf16[64,6,3584]{2,1,0:T(8,128)(2,1)S(1)} %get-tuple-element.10), channel_id=1, replica_groups=mesh['expert'=64,'dp'=2] {'expert'}, dimensions={0} | all-to-all | bytes 5505024 | tf_op jit(solution)/shard_map/all_to_all | solution.py:49
  89.2 10.3 %all-to-all-start.4 = ((bf16[64,6,3584]{2,1,0:T(8,128)(2,1)}), bf16[64,6,3584]{2,1,0:T(8,128)(2,1)}, u32[]{:S(2)}, u32[]{:S(2)}) async-start(bf16[64,6,3584]{2,1,0:T(8,128)(2,1)} %get-tuple-element.11), calls=%async_computation.4 | async-start | bytes 7340032 | tf_op jit(solution)/shard_map/all_to_all | solution.py:56
  99.6 7.3 %all_to_all.79 = bf16[384,2,1792]{2,1,0:T(2,128)(2,1)} reshape(bf16[64,6,3584]{2,1,0:T(8,128)(2,1)} %all_to_all.107) | data formatting | bytes 5505024 | tf_op jit(solution)/shard_map/all_to_all | solution.py:75
  106.8 8.6 %copy.19 = bf16[384,2,1792]{0,2,1:T(8,128)(2,1)} copy(bf16[384,2,1792]{2,1,0:T(2,128)(2,1)} %all_to_all.79) | data formatting | bytes 5505024 | tf_op jit(solution)/shard_map/all_to_all | solution.py:75
  115.4 32.5 %all-to-all-done.4 = bf16[64,6,3584]{2,1,0:T(8,128)(2,1)} async-done(((bf16[64,6,3584]{2,1,0:T(8,128)(2,1)}), bf16[64,6,3584]{2,1,0:T(8,128)(2,1)}, u32[]{:S(2)}, u32[]{:S(2)}) %all-to-all-start.4) | async-done | bytes 2752544 | tf_op jit(solution)/shard_map/all_to_all | solution.py:56
  152.9 7.3 %all_to_all.84 = bf16[384,2,1792]{2,1,0:T(2,128)(2,1)} reshape(bf16[64,6,3584]{2,1,0:T(8,128)(2,1)} %all-to-all-done.4) | data formatting | bytes 5505024 | tf_op jit(solution)/shard_map/all_to_all | solution.py:76
  163.8 22.1 %all-to-all-done.3 = bf16[384,2,1792]{0,2,1:T(8,128)(2,1)} async-done(((bf16[384,2,1792]{0,2,1:T(8,128)(2,1)}), bf16[384,2,1792]{0,2,1:T(8,128)(2,1)}, u32[]{:S(2)}, u32[]{:S(2)}) %all-to-all-start.3) | async-done | bytes 2752544 | tf_op jit(solution)/shard_map/all_to_all | solution.py:75
  195.9 6.0 %fusion.16 = bf16[768,1024]{1,0:T(8,128)(2,1)S(1)} fusion(bf16[768,1792]{1,0:T(8,128)(2,1)} %bitcast.70, bf16[1,1792,1024]{2,1,0:T(8,128)(2,1)} %param.11), kind=kOutput, calls=%fused_computation.30 | convolution fusion | flops 2819358720 | bytes 7995392 | tf_op jit(solution)/shard_map/dot_general | solution.py:87
  206.0 17.2 %all-to-all-done.5 = bf16[384,2,1792]{2,0,1:T(8,128)(2,1)} async-done(((bf16[384,2,1792]{2,0,1:T(8,128)(2,1)}), bf16[384,2,1792]{2,0,1:T(8,128)(2,1)}, u32[]{:S(2)}, u32[]{:S(2)}) %all-to-all-start.5) | async-done | bytes 2752544 | tf_op jit(solution)/shard_map/all_to_all | solution.py:76
  235.1 13.5 %all_to_all.108 = bf16[64,1,6]{2,1,0:T(2,128)(2,1)S(1)} all-to-all(bf16[64,1,6]{2,1,0:T(2,128)(2,1)S(1)} %all_to_all.95), channel_id=1, replica_groups=mesh['expert'=64,'dp'=2] {'expert'}, dimensions={0} | all-to-all | bytes 1536 | tf_op jit(solution)/shard_map/all_to_all | solution.py:63
  257.9 36.4 %reduce-scatter.2.cloned.1.call-done = bf16[384,3072]{1,0:T(8,128)(2,1)} async-done(((bf16[768,3072]{1,0:T(8,128)(2,1)}), bf16[384,3072]{1,0:T(8,128)(2,1)}) %reduce-scatter.2.cloned.1.call-update) | async-done | bytes 2359312 | tf_op jit(solution)/shard_map/reduce_scatter | solution.py:84
  304.6 35.8 %all-gather.4.cloned.1.call-done = bf16[768,1024]{1,0:T(8,128)(2,1)} async-done(((bf16[384,1024]{1,0:T(8,128)(2,1)}), bf16[768,1024]{1,0:T(8,128)(2,1)}) %all-gather.4.cloned.1.call-update) | async-done | bytes 1572880 | tf_op jit(solution)/shard_map/all_gather | solution.py:102
  340.4 8.0 %fusion.3 = f32[768,1792]{1,0:T(8,128)} fusion(bf16[768,1024]{1,0:T(8,128)(2,1)} %all-gather.4.cloned.1.call-done, bf16[1,1792,1024]{2,1,0:T(8,128)(2,1)} %param.12), kind=kOutput, calls=%fused_computation.16 | convolution fusion | flops 2818572288 | bytes 10747904 | tf_op jit(solution)/shard_map/rf,df->rd/dot_general | solution.py:119
  348.4 7.2 %add_convert_fusion = bf16[768,1792]{1,0:T(8,128)(2,1)} fusion(f32[768,1792]{1,0:T(8,128)} %fusion.3, bf16[768,1024]{1,0:T(8,128)(2,1)S(1)} %bitcast.74, bf16[1,1792,1024]{2,1,0:T(8,128)(2,1)} %param.11), kind=kOutput, calls=%fused_computation.9 | convolution fusion | flops 2821324800 | bytes 13500416 | tf_op jit(solution)/shard_map/rf,df->rd/dot_general | solution.py:116
  362.1 20.8 %all-gather.6.cloned.1.call-done = bf16[768,1024]{1,0:T(8,128)(2,1)} async-done(((bf16[384,1024]{1,0:T(8,128)(2,1)}), bf16[768,1024]{1,0:T(8,128)(2,1)}) %all-gather.6.cloned.1.call-update) | async-done | bytes 1572880 | tf_op jit(solution)/shard_map/all_gather | solution.py:98
  382.9 6.5 %multiply_reduce_fusion = f32[768]{0:T(1024)S(1)} fusion(bf16[768,1792]{1,0:T(8,128)(2,1)} %bitcast.9, bf16[768,1024]{1,0:T(8,128)(2,1)} %all-gather.6.cloned.1.call-done, bf16[1,1792,1024]{2,1,0:T(8,128)(2,1)} %param.13), kind=kOutput, calls=%fused_computation.8 | convolution fusion | flops 2822700288 | bytes 7998464 | tf_op jit(solution)/shard_map/rf,df->rd/dot_general | solution.py:122
  389.4 13.4 %all-reduce.1 = bf16[768]{0:T(1024)(128)(2,1)S(1)} all-reduce(f32[768]{0:T(1024)S(1)} %multiply_reduce_fusion), channel_id=3, replica_groups=mesh['expert'=64,'dp'=2] {'dp'}, use_global_device_ids=true, to_apply=%region_6.7.clone | all-reduce | flops 768 | bytes 4608
  403.7 10.6 %all-to-all-start.9 = ((bf16[64,1,6]{2,1,0:T(2,128)(2,1)}), bf16[64,1,6]{2,1,0:T(2,128)(2,1)S(1)}, u32[]{:S(2)}, u32[]{:S(2)}) async-start(bf16[64,1,6]{2,1,0:T(2,128)(2,1)} %all_to_all.96), calls=%async_computation.10 | async-start | bytes 65536 | tf_op jit(solution)/shard_map/all_to_all | solution.py:136
  414.3 6.1 %copy.22 = bf16[384,2,1792]{2,1,0:T(2,128)(2,1)} copy(bf16[384,2,1792]{2,0,1:T(8,128)(2,1)} %bitcast.14) | data formatting | bytes 5505024 | tf_op jit(solution)/shard_map/all_to_all | solution.py:127
  420.5 7.6 %reshape.80 = bf16[64,6,3584]{2,1,0:T(8,128)(2,1)} reshape(bf16[384,2,1792]{2,1,0:T(2,128)(2,1)} %copy.22) | data formatting | bytes 5505024 | tf_op jit(solution)/shard_map/reshape | solution.py:130
  428.1 10.5 %all-to-all-start.8 = ((bf16[64,6,3584]{2,1,0:T(8,128)(2,1)}), bf16[64,6,3584]{2,1,0:T(8,128)(2,1)}, u32[]{:S(2)}, u32[]{:S(2)}) async-start(bf16[64,6,3584]{2,1,0:T(8,128)(2,1)} %reshape.80), calls=%async_computation.9 | async-start | bytes 7340032 | tf_op jit(solution)/shard_map/all_to_all | solution.py:129
  438.6 43.8 %all-gather = bf16[2,1,384]{2,1,0:T(2,128)(2,1)S(1)} all-gather(bf16[1,1,384]{2,1,0:T(2,128)(2,1)S(1)} %reshape.145), channel_id=1, replica_groups=mesh['expert'=64,'dp'=2] {'dp'}, dimensions={0}, use_global_device_ids=true | all-gather | bytes 2304 | tf_op jit(solution)/shard_map/all_gather | solution.py:103
  482.5 6.4 %fusion.13 = bf16[1,1792,1024]{2,1,0:T(8,128)(2,1)} fusion(bf16[2,384,1024]{2,1,0:T(8,128)(2,1)S(1)} %all-to-all-done.6, bf16[384,2,1792]{0,2,1:T(8,128)(2,1)} %all-to-all-done.3), kind=kOutput, calls=%fused_computation.28 | convolution fusion | flops 2820407296 | bytes 7995392 | tf_op jit(solution)/shard_map/rd,rf->df/dot_general | solution.py:109
  493.4 6.4 %fusion.12 = bf16[1,1792,1024]{2,1,0:T(8,128)(2,1)} fusion(bf16[768,1792]{1,0:T(8,128)(2,1)} %bitcast.9, bf16[768,1024]{1,0:T(8,128)(2,1)S(1)} %copy-done.9, f32[768]{0:T(1024)S(1)} %reshape.147), kind=kOutput, calls=%fused_computation.27 | convolution fusion | flops 2822766592 | bytes 7998464 | tf_op jit(solution)/shard_map/rd,rf->df/dot_general | solution.py:115
  (88 shorter events, 105.9 us)
Async XLA Ops:
  7.2 3.5 copy-start
  14.6 5.5 %copy-start.3 = (bf16[128,3584]{1,0:T(8,128)(2,1)S(1)}, bf16[128,3584]{1,0:T(8,128)(2,1)}, u32[]{:S(2)}) copy-start(bf16[128,3584]{1,0:T(8,128)(2,1)} %param.8) | copy-start | bytes 2752516
  89.2 58.7 %all-to-all-start.4 = ((bf16[64,6,3584]{2,1,0:T(8,128)(2,1)}), bf16[64,6,3584]{2,1,0:T(8,128)(2,1)}, u32[]{:S(2)}, u32[]{:S(2)}) async-start(bf16[64,6,3584]{2,1,0:T(8,128)(2,1)} %get-tuple-element.11), calls=%async_computation.4 | async-start | bytes 7340032 | tf_op jit(solution)/shard_map/all_to_all | solution.py:56
  147.9 38.0 %all-to-all-start.3 = ((bf16[384,2,1792]{0,2,1:T(8,128)(2,1)}), bf16[384,2,1792]{0,2,1:T(8,128)(2,1)}, u32[]{:S(2)}, u32[]{:S(2)}) async-start(bf16[384,2,1792]{0,2,1:T(8,128)(2,1)} %copy.19), calls=%async_computation.3 | async-start | bytes 5505024 | tf_op jit(solution)/shard_map/all_to_all | solution.py:75
  185.9 37.4 %all-to-all-start.5 = ((bf16[384,2,1792]{2,0,1:T(8,128)(2,1)}), bf16[384,2,1792]{2,0,1:T(8,128)(2,1)}, u32[]{:S(2)}, u32[]{:S(2)}) async-start(bf16[384,2,1792]{2,0,1:T(8,128)(2,1)} %copy.21), calls=%async_computation.5 | async-start | bytes 5505024 | tf_op jit(solution)/shard_map/all_to_all | solution.py:76
  191.1 103.3 %reduce-scatter.2.cloned.1.call-start = ((), (), s32[]{:S(2)}) async-start(), calls=%async_computation.11 | async-start | bytes 7077888 | tf_op jit(solution)/shard_map/reduce_scatter | solution.py:84
  195.9 6.0 %copy-start.4 = (bf16[2,384,1792]{2,1,0:T(8,128)(2,1)S(1)}, bf16[2,384,1792]{2,1,0:T(8,128)(2,1)}, u32[]{:S(2)}) copy-start(bf16[2,384,1792]{2,1,0:T(8,128)(2,1)} %copy.20) | copy-start | bytes 8257540
  195.9 6.0 %copy-start.7 = (bf16[1,1792,1024]{2,1,0:T(8,128)(2,1)S(1)}, bf16[1,1792,1024]{2,1,0:T(8,128)(2,1)}, u32[]{:S(2)}) copy-start(bf16[1,1792,1024]{2,1,0:T(8,128)(2,1)} %param.12) | copy-start | bytes 11010052
  223.3 6.0 %copy-start.6 = (bf16[768,1024]{1,0:T(8,128)(2,1)S(1)}, bf16[768,1024]{1,0:T(8,128)(2,1)}, u32[]{:S(2)}) copy-start(bf16[768,1024]{1,0:T(8,128)(2,1)} %fusion.19) | copy-start | bytes 4718596
  231.6 0.7 copy-start.2
  250.7 7.0 %all-to-all-start.1 = ((bf16[2,2,192]{2,1,0:T(2,128)(2,1)}), bf16[2,2,192]{2,1,0:T(2,128)(2,1)S(1)}, u32[]{:S(2)}, u32[]{:S(2)}) async-start(bf16[2,2,192]{2,1,0:T(2,128)(2,1)} %reshape.158), calls=%async_computation.1 | async-start | bytes 4096 | tf_op jit(solution)/shard_map/all_to_all | solution.py:77
  253.9 86.5 %all-gather.4.cloned.1.call-start = ((), (), s32[]{:S(2)}) async-start(), calls=%async_computation.12 | async-start | bytes 2359296 | tf_op jit(solution)/shard_map/all_gather | solution.py:102
  300.1 48.2 %all-to-all-start.6 = ((bf16[2,384,1024]{2,1,0:T(8,128)(2,1)}), bf16[2,384,1024]{2,1,0:T(8,128)(2,1)S(1)}, u32[]{:S(2)}, u32[]{:S(2)}) async-start(bf16[2,384,1024]{2,1,0:T(8,128)(2,1)} %pad_maximum_fusion.1), calls=%async_computation.7 | async-start | bytes 3145728 | tf_op jit(solution)/shard_map/all_to_all | solution.py:100
  303.8 79.1 %all-gather.6.cloned.1.call-start = ((), (), s32[]{:S(2)}) async-start(), calls=%async_computation.13 | async-start | bytes 2359296 | tf_op jit(solution)/shard_map/all_gather | solution.py:98
  355.6 5.2 %copy-start.10 = (u32[128]{0:T(128)S(1)}, u32[128]{0:T(128)}, u32[]{:S(2)}) copy-start(u32[128]{0:T(128)} %constant.54) | copy-start | bytes 1540
  355.6 48.1 %all-to-all-start.7 = ((bf16[2,384,1792]{2,1,0:T(8,128)(2,1)}), bf16[2,384,1792]{2,1,0:T(8,128)(2,1)}, u32[]{:S(2)}, u32[]{:S(2)}) async-start(bf16[2,384,1792]{2,1,0:T(8,128)(2,1)} %bitcast.73), calls=%async_computation.8 | async-start | bytes 5505024 | tf_op jit(solution)/shard_map/all_to_all | solution.py:127
  403.7 24.4 %all-to-all-start.9 = ((bf16[64,1,6]{2,1,0:T(2,128)(2,1)}), bf16[64,1,6]{2,1,0:T(2,128)(2,1)S(1)}, u32[]{:S(2)}, u32[]{:S(2)}) async-start(bf16[64,1,6]{2,1,0:T(2,128)(2,1)} %all_to_all.96), calls=%async_computation.10 | async-start | bytes 65536 | tf_op jit(solution)/shard_map/all_to_all | solution.py:136
  428.1 73.8 %all-to-all-start.8 = ((bf16[64,6,3584]{2,1,0:T(8,128)(2,1)}), bf16[64,6,3584]{2,1,0:T(8,128)(2,1)}, u32[]{:S(2)}, u32[]{:S(2)}) async-start(bf16[64,6,3584]{2,1,0:T(8,128)(2,1)} %reshape.80), calls=%async_computation.9 | async-start | bytes 7340032 | tf_op jit(solution)/shard_map/all_to_all | solution.py:129
  482.5 6.4 %copy-start.5 = (bf16[2,384,1792]{2,1,0:T(8,128)(2,1)S(1)}, bf16[2,384,1792]{2,1,0:T(8,128)(2,1)}, u32[]{:S(2)}) copy-start(bf16[2,384,1792]{2,1,0:T(8,128)(2,1)} %copy.20) | copy-start | bytes 8257540
  482.5 6.4 %copy-start.8 = (bf16[768,1024]{1,0:T(8,128)(2,1)S(1)}, bf16[768,1024]{1,0:T(8,128)(2,1)}, u32[]{:S(2)}) copy-start(bf16[768,1024]{1,0:T(8,128)(2,1)} %all-gather.4.cloned.1.call-done) | copy-start | bytes 4718596
  488.9 4.5 copy-start.9
  501.8 10.7 %copy-start.1 = (bf16[128,3584]{1,0:T(8,128)(2,1)S(1)}, bf16[128,3584]{1,0:T(8,128)(2,1)}, u32[]{:S(2)}) copy-start(bf16[128,3584]{1,0:T(8,128)(2,1)} %param.7) | copy-start | bytes 2752516
Sparse Core Ops, SparseCore 0:
  231.7 62.5 reduce-scatter.1
  299.0 41.3 all-gather.3
  342.7 40.1 all-gather.5
